TPU v7x, 256 devices: a whole 4x4x8 slice. The times are simulated.
256 devices in a mesh: dp: 16 (over x_hi, z), expert: 16 (over y, x_lo, core).
Axes of the slice: x: 4 (x_hi: 2, x_lo: 2; x = x_hi * 2 + x_lo), y: 4, z: 8, core: 2. Of those that a mesh axis runs over, the one named last changes fastest.
Arguments:
- tokens: bfloat16 [65536, 4096], P(('dp', 'expert')), may hold values from -6 to 6
- chosen: int32 [256, 16, 32], P(('dp', 'expert')), may hold values from 0 to 255, as said below
- gates: float32 [256, 16, 32], P(('dp', 'expert')), may hold values from 0.25 to 1
- w_gate: bfloat16 [16, 4096, 768], P('expert', 'dp'), may hold values from -0.09375 to 0.09375
- w_up: bfloat16 [16, 4096, 768], P('expert', 'dp'), may hold values from -0.09375 to 0.09375
- w_down: bfloat16 [16, 768, 4096], P('expert', None, 'dp'), may hold values from -0.21875 to 0.21875
Outputs:
- layer_out: bfloat16 [65536, 4096], P(('dp', 'expert'))
Inputs may be any that keep to these rules, and one draw needn't show every extreme that they name: `chosen`: for each slab and expert the 32 picked rows are distinct rows of the slab; every expert picks exactly 32 rows in every slab.
All inputs are finite; a program needn't handle non-finite values.
Results may differ from a plain program's by a relative error of at most 0.0049.
Values may be sent and summed in bfloat16 or wider, within the bound.
A program may use at most 128 MiB of HBM per device.

v0:
```python
import jax
import jax.numpy as jnp
from jax import lax
from jax.sharding import PartitionSpec as P


def shards(tokens, chosen, gates, w_gate, w_up, w_down):
    experts = chosen.shape[1]
    per_slab = chosen.shape[2]
    model_width = tokens.shape[1]
    pick_rows = chosen[0].reshape(-1)
    picked = jnp.take(tokens, pick_rows, axis=0).reshape(experts, per_slab, model_width)
    arrived = lax.all_to_all(picked, "expert", split_axis=0, concat_axis=0, tiled=True)
    inputs = arrived.reshape(-1, model_width)
    full_gate, full_up = (
        lax.all_gather(w_gate[0], "dp", axis=0, tiled=True),
        lax.all_gather(w_up[0], "dp", axis=0, tiled=True),
    )
    gate_part = jnp.dot(inputs, full_gate, preferred_element_type=jnp.float32)
    up_part = jnp.dot(inputs, full_up, preferred_element_type=jnp.float32)
    hidden = (jax.nn.silu(gate_part) * up_part).astype(jnp.bfloat16)
    expert_out = jnp.dot(
        hidden,
        lax.all_gather(w_down[0], "dp", axis=1, tiled=True),
        preferred_element_type=jnp.float32,
    )
    returned = lax.all_to_all(
        expert_out.reshape(experts, per_slab, model_width),
        "expert",
        split_axis=0,
        concat_axis=0,
        tiled=True,
    )
    weighted = gates[0][:, :, None] * returned
    combined = (
        jnp.zeros((tokens.shape[0], model_width), jnp.float32)
        .at[pick_rows]
        .add(weighted.reshape(-1, model_width))
    )
    return combined.astype(jnp.bfloat16)


def solution(mesh):
    in_specs = (
        P(("dp", "expert"), None),
        P(("dp", "expert"), None, None),
        P(("dp", "expert"), None, None),
        P("expert", "dp", None),
        P("expert", "dp", None),
        P("expert", None, "dp"),
    )
    out_specs = P(("dp", "expert"), None)
    return jax.shard_map(shards, mesh=mesh, in_specs=in_specs, out_specs=out_specs, check_vma=False)
```

profile of v0, /device:TPU:1, one launch (start us, length us, event | category | flops | bytes accessed | tf_op | source)
XLA Modules:
  0.0 526.5 jit_solution(6415197587071154605)
XLA Ops:
  6.5 0.0 copy-start
  6.5 0.0 all-gather.7.cloned.1.call-start
  6.5 0.7 all-gather.7.cloned.1.call-update
  7.3 0.0 all-gather.11.cloned.1.call-start
  7.3 0.7 all-gather.11.cloned.1.call-update
  8.0 0.0 all-gather.9.cloned.1.call-start
  8.1 0.7 all-gather.9.cloned.1.call-update
  8.7 0.8 reshape_squeeze.5
  9.5 0.0 copy-done
  9.5 0.0 copy-start.2
  9.6 4.4 gather_fusion
  14.0 0.0 copy-done.2
  14.0 2.6 broadcast_select_fusion
  16.6 63.2 %all_to_all.10 = bf16[16,32,4096]{2,1,0:T(8,128)(2,1)} all-to-all(bf16[16,32,4096]{2,1,0:T(8,128)(2,1)S(1)} %broadcast_select_fusion), channel_id=1, replica_groups=mesh['dp'=16,'expert'=16] {'expert'}, dimensions={0} | all-to-all | bytes 8388608 | tf_op jit(solution)/shard_map/all_to_all | solution.py:13
  79.8 59.4 %all-gather.7.cloned.1.call-done = bf16[1,4096,768]{2,1,0:T(8,128)(2,1)} async-done(((bf16[1,256,768]{2,1,0:T(8,128)(2,1)}), bf16[1,4096,768]{2,1,0:T(8,128)(2,1)}) %all-gather.7.cloned.1.call-update) | async-done | bytes 6291472 | tf_op jit(solution)/shard_map/all_gather | solution.py:16
  139.2 7.0 %fusion.4 = f32[512,768]{1,0:T(8,128)S(1)} fusion(bf16[512,4096]{1,0:T(8,128)(2,1)} %bitcast.28, bf16[1,4096,768]{2,1,0:T(8,128)(2,1)} %all-gather.7.cloned.1.call-done), kind=kOutput, calls=%fused_computation.6 | convolution fusion | flops 3221225472 | bytes 12058624 | tf_op jit(solution)/shard_map/dot_general | solution.py:19
  146.2 114.5 %all-gather.11.cloned.1.call-done = bf16[1,768,4096]{2,1,0:T(8,128)(2,1)} async-done(((bf16[1,768,256]{2,1,0:T(8,128)(2,1)}), bf16[1,768,4096]{2,1,0:T(8,128)(2,1)}) %all-gather.11.cloned.1.call-update) | async-done | bytes 6291472 | tf_op jit(solution)/shard_map/all_gather | solution.py:24
  260.7 117.1 %all-gather.9.cloned.1.call-done = bf16[1,4096,768]{2,1,0:T(8,128)(2,1)} async-done(((bf16[1,256,768]{2,1,0:T(8,128)(2,1)}), bf16[1,4096,768]{2,1,0:T(8,128)(2,1)}) %all-gather.9.cloned.1.call-update) | async-done | bytes 6291472 | tf_op jit(solution)/shard_map/all_gather | solution.py:17
  377.8 17.8 %fusion = f32[512,4096]{1,0:T(8,128)} fusion(bf16[1,768,4096]{2,1,0:T(8,128)(2,1)} %all-gather.11.cloned.1.call-done, f32[512,768]{1,0:T(8,128)S(1)} %fusion.4, bf16[512,4096]{1,0:T(8,128)(2,1)} %bitcast.29, bf16[1,4096,768]{2,1,0:T(8,128)(2,1)} %all-gather.9.cloned.1.call-done), kind=kOutput, calls=%fused_computation.2 | convolution fusion | flops 6444810240 | bytes 26738688 | tf_op jit(solution)/shard_map/dot_general | solution.py:22
  395.6 0.0 copy-start.3
  395.6 100.1 %all_to_all.11 = f32[16,32,4096]{2,1,0:T(8,128)S(1)} all-to-all(f32[16,32,4096]{2,1,0:T(8,128)} %bitcast.26), channel_id=1, replica_groups=mesh['dp'=16,'expert'=16] {'expert'}, dimensions={0} | all-to-all | bytes 16777216 | tf_op jit(solution)/shard_map/all_to_all | solution.py:27
  495.7 0.0 copy-done.3
  495.7 4.2 broadcast_multiply_fusion
  499.9 0.0 copy-start.1
  499.9 16.3 %scatter_custom_fusion = f32[256,4096]{1,0:T(8,128)} fusion(s32[512]{0:T(512)S(1)} %bitcast.32, f32[512,4096]{1,0:T(8,128)} %bitcast.27, f32[]{:T(128)} %constant.7.clone.1), kind=kCustom, calls=%fused_computation.10 | custom fusion | flops 2097152 | bytes 4194816 | tf_op jit(solution)/shard_map/scatter-add | solution.py:38
  516.2 3.8 convert_element_type.7
  520.0 0.0 copy-done.1
  (3 shorter events, 0.0 us)
Async XLA Ops:
  6.5 3.0 copy-start
  6.5 132.6 %all-gather.7.cloned.1.call-start = ((), (), s32[]{:S(2)}) async-start(), calls=%async_computation.2 | async-start | bytes 6684672 | tf_op jit(solution)/shard_map/all_gather | solution.py:16
  7.3 253.5 %all-gather.11.cloned.1.call-start = ((), (), s32[]{:S(2)}) async-start(), calls=%async_computation.4 | async-start | bytes 6684672 | tf_op jit(solution)/shard_map/all_gather | solution.py:24
  8.0 369.8 %all-gather.9.cloned.1.call-start = ((), (), s32[]{:S(2)}) async-start(), calls=%async_computation.3 | async-start | bytes 6684672 | tf_op jit(solution)/shard_map/all_gather | solution.py:17
  9.5 4.4 copy-start.2
  395.6 100.1 %copy-start.3 = (f32[1,16,32]{2,1,0:T(8,128)S(1)}, f32[1,16,32]{2,1,0:T(8,128)}, u32[]{:S(2)}) copy-start(f32[1,16,32]{2,1,0:T(8,128)} %param.8) | copy-start | bytes 6148
  499.9 20.1 %copy-start.1 = (bf16[256,4096]{1,0:T(8,128)(2,1)S(1)}, bf16[256,4096]{1,0:T(8,128)(2,1)}, u32[]{:S(2)}) copy-start(bf16[256,4096]{1,0:T(8,128)(2,1)} %param.6) | copy-start | bytes 6291460
Sparse Core Ops, SparseCore 0:
  9.9 129.1 all-gather.6
  141.6 119.0 all-gather.10
  263.3 114.4 all-gather.8
where the time goes:
time: 527 us
  waiting for transfers between devices  293 us (56%)
  blocking collectives  163 us (31%)
  other arithmetic  26.9 us (5%)
  matrix products  24.9 us (5%)
  between operations  13.1 us (2%)
    all_gather x1, waiting for transfers between devices, shards(): lax.all_gather(w_up[0], 'dp', axis=0, tiled=True)  117 us
    all_gather x1, waiting for transfers between devices, shards(): lax.all_gather(w_down[0], 'dp', axis=1, tiled=True)  115 us
    all_to_all x1, blocking collectives, shards(): lax.all_to_all(expert_out.reshape(experts, per_slab, model_width), 'exper...  100 us
    all_to_all x1, blocking collectives, shards(): lax.all_to_all(picked, 'expert', split_axis=0, concat_axis=0, tiled=True)  63.2 us
    all_gather x1, waiting for transfers between devices, shards(): lax.all_gather(w_gate[0], 'dp', axis=0, tiled=True)  59.4 us
    dot_general x1, matrix products, shards(): jnp.dot(hidden, lax.all_gather(w_down[0], 'dp', axis=1, tiled=True), pref...  17.8 us
    scatter-add x1, other arithmetic, shards(): combined = jnp.zeros((tokens.shape[0], model_width), jnp.float32).at[pick...  16.3 us
  transfers between devices with their start and end apart: 3, of which 3 were waited for; matrix products, arithmetic and copies ran while one was open for 3% of the time, Pallas kernels for 0%

commit v1 on v0

v1 whole, which is shorter than its diff:
```python
import jax
import jax.numpy as jnp
from jax import lax
from jax.experimental import pallas as pl
from jax.experimental.pallas import tpu as pltpu
from jax.sharding import PartitionSpec as P

MESH = pl.DeviceIdType.MESH
OFFSET = (0, 1, -1, 2, -2, 3, -3, 4)
PEERS = 16
CHUNKS = 4
SLOTS = 8


def moe_kernel(
    tok, cho, gat, wg, wu, wd, o,
    onehot, gcol, gmix, stage, xin, wgu, wdn, acc, hid, ost, ret,
    tok_send, tok_recv, ret_send, ret_recv,
    slot_recv, ring_send, sib_send, sib_recv, cross_send,
):
    dp, ex = lax.axis_index("dp"), lax.axis_index("expert")
    x_hi, z = dp // 8, dp % 8
    y, x_lo, c = ex // 4, (ex // 2) % 2, ex % 2
    x = x_hi * 2 + x_lo
    per = cho.shape[2]
    rows = PEERS * per
    wide = wg.shape[1]

    def device(xx, yy, zz, cc):
        xx, yy, zz = xx % 4, yy % 4, zz % 8
        return ((xx // 2) * 8 + zz, yy * 4 + (xx % 2) * 2 + cc)

    def shard_of(slot, p):
        column = c if p == 0 else 1 - c
        return column * 8 + (z + OFFSET[slot] + 8) % 8

    up, down = device(x, y, z + 1, c), device(x, y, z + 7, c)
    sibling = device(x, y, z, 1 - c)
    across = device(x + 2, y, z, 1 - c)
    native = c == x_hi

    barrier = pltpu.get_barrier_semaphore()

    def greet(r, carry):
        pl.semaphore_signal(
            barrier, inc=1, device_id=device(x + r % 4, y + r // 4, z, c), device_id_type=MESH
        )
        return carry

    lax.fori_loop(1, PEERS, greet, 0)
    for other in (up, down, sibling, across):
        pl.semaphore_signal(barrier, inc=1, device_id=other, device_id_type=MESH)

    def weight(k, slot, p):
        return wdn.at[slot, p] if k == 2 else wgu.at[k, slot, p]

    sources = (wg.at[0], wu.at[0], wd.at[0])

    @pl.when(native)
    def _():
        for k in range(3):
            pltpu.make_async_copy(sources[k], weight(k, 0, 0), slot_recv.at[k, 0]).start()

    eye = lax.broadcasted_iota(jnp.int32, (per, per), 0) == lax.broadcasted_iota(
        jnp.int32, (per, per), 1
    )
    token_id = lax.broadcasted_iota(jnp.int32, (per, onehot.shape[1]), 1).astype(jnp.float32)
    for r in range(PEERS):
        xx, yy = (x + r % 4) % 4, (y + r // 4) % 4
        e = yy * 4 + (xx % 2) * 2 + xx // 2
        picks = cho[0, pl.ds(e, 1), :].astype(jnp.float32)
        weights = gat[0, pl.ds(e, 1), :]
        pick_col = jnp.sum(jnp.where(eye, picks, 0.0), axis=1, keepdims=True)
        gate_col = jnp.sum(jnp.where(eye, weights, 0.0), axis=1, keepdims=True)
        hit = token_id == pick_col
        onehot[pl.ds(r * per, per), :] = jnp.where(hit, 1.0, 0.0).astype(jnp.bfloat16)
        gcol[pl.ds(r * per, per), :] = jnp.where(hit, gate_col, 0.0)

    pl.semaphore_wait(barrier, PEERS - 1 + 4)

    def cross(k):
        return pltpu.make_async_remote_copy(
            src_ref=sources[k], dst_ref=weight(k, 0, 0), send_sem=cross_send.at[k],
            recv_sem=slot_recv.at[k, 0], device_id=across, device_id_type=MESH,
        )

    @pl.when(jnp.logical_not(native))
    def _():
        for k in range(2):
            cross(k).start()

    def arrived(k, slot):
        pltpu.make_async_copy(
            weight(k, slot, 0), weight(k, slot, 0), slot_recv.at[k, slot]
        ).wait()

    def to_sibling(k, slot):
        return pltpu.make_async_remote_copy(
            src_ref=weight(k, slot, 0), dst_ref=weight(k, slot, 1), send_sem=sib_send.at[k, slot],
            recv_sem=sib_recv.at[k, slot], device_id=sibling, device_id_type=MESH,
        )

    def hop(k, src, dst, target):
        return pltpu.make_async_remote_copy(
            src_ref=weight(k, src, 0), dst_ref=weight(k, dst, 0), send_sem=ring_send.at[k, dst],
            recv_sem=slot_recv.at[k, dst], device_id=target, device_id_type=MESH,
        )

    def last_hop(k):
        return hop(k, 6 - c, 7, device(x, y, z + 1 + 6 * c, c))

    def spread(k, slot):
        if slot == 0:
            hop(k, 0, 2, up).start()
            hop(k, 0, 1, down).start()
        elif slot in (1, 3):
            hop(k, slot, slot + 2, down).start()
        elif slot in (2, 4):
            hop(k, slot, slot + 2, up).start()
        if slot == 5:

            @pl.when(c == 1)
            def _():
                last_hop(k).start()

        if slot == 6:

            @pl.when(c == 0)
            def _():
                last_hop(k).start()

        to_sibling(k, slot).start()

    @pl.when(native)
    def _():
        for k in range(2):
            arrived(k, 0)
            spread(k, 0)

    def send_tokens(g):
        for i in range(4):
            j = shard_of(2 * g + i // 2, i % 2)
            stage[g, :, pl.ds(i * 256, 256)] = jnp.dot(
                onehot[...],
                tok[:, pl.ds(pl.multiple_of(j * 256, 256), 256)],
                preferred_element_type=jnp.float32,
            ).astype(jnp.bfloat16)

        def send(r, carry):
            block = pl.ds(pl.multiple_of(r * per, per), per)
            pltpu.make_async_remote_copy(
                src_ref=stage.at[g, block], dst_ref=xin.at[g, block], send_sem=tok_send.at[g],
                recv_sem=tok_recv.at[g], device_id=device(x + r % 4, y + r // 4, z, c),
                device_id_type=MESH,
            ).start()
            return carry

        lax.fori_loop(1, PEERS, send, 0)
        xin[g, pl.ds(0, per), :] = stage[g, pl.ds(0, per), :]

    for g in range(CHUNKS):
        send_tokens(g)

    @pl.when(jnp.logical_not(native))
    def _():
        cross(2).start()
        for k in range(2):
            arrived(k, 0)
            spread(k, 0)

    mixed = gcol[...].T
    high = mixed.astype(jnp.bfloat16)
    gmix[0] = high
    gmix[1] = (mixed - high.astype(jnp.float32)).astype(jnp.bfloat16)

    def from_sibling(k, slot):
        pltpu.make_async_copy(
            weight(k, slot, 1), weight(k, slot, 1), sib_recv.at[k, slot]
        ).wait()

    others = pl.ds(per, rows - per)
    for g in range(CHUNKS):
        step_slots = (2 * g + 1, 2 * g + 2) if g < 3 else (7,)
        for slot in step_slots:
            for k in range(2):
                arrived(k, slot)
                spread(k, slot)
        if g == 2:
            arrived(2, 0)
            spread(2, 0)
        for slot in (2 * g, 2 * g + 1):
            for k in range(2):
                from_sibling(k, slot)
        pltpu.make_async_copy(xin.at[g, others], xin.at[g, others], tok_recv.at[g]).wait()

        def multiply(n, carry):
            k, tile = n // 3, n % 3
            part = wgu[k, pl.ds(2 * g, 2), :, :, pl.ds(pl.multiple_of(tile * 256, 256), 256)]
            product = jnp.dot(
                xin[g], part.reshape(4 * wide, 256), preferred_element_type=jnp.float32
            )
            if g == 0:
                acc[n] = product
            else:
                acc[n] += product
            return carry

        lax.fori_loop(0, 6, multiply, 0)

    for tile in range(3):
        gate_part = acc[tile]
        hid[:, pl.ds(tile * 256, 256)] = (
            gate_part / (1.0 + jnp.exp(-gate_part)) * acc[3 + tile]
        ).astype(jnp.bfloat16)

    for slot in range(SLOTS):
        if slot > 0:
            arrived(2, slot)
            spread(2, slot)
        from_sibling(2, slot)
        for p in range(2):
            ost[slot, :, pl.ds(p * 256, 256)] = jnp.dot(
                hid[...], wdn[slot, p], preferred_element_type=jnp.float32
            ).astype(jnp.bfloat16)

        def give_back(r, carry):
            block = pl.ds(pl.multiple_of(r * per, per), per)
            pltpu.make_async_remote_copy(
                src_ref=ost.at[slot, block], dst_ref=ret.at[slot, block],
                send_sem=ret_send.at[slot], recv_sem=ret_recv.at[slot],
                device_id=device(x + 4 - r % 4, y + 4 - r // 4, z, c), device_id_type=MESH,
            ).start()
            return carry

        lax.fori_loop(1, PEERS, give_back, 0)
        ret[slot, pl.ds(0, per), :] = ost[slot, pl.ds(0, per), :]

    for slot in range(SLOTS):
        pltpu.make_async_copy(
            ret.at[slot, others], ret.at[slot, others], ret_recv.at[slot]
        ).wait()
        for p in range(2):
            half = ret[slot, :, pl.ds(p * 256, 256)]
            j = shard_of(slot, p)
            o[:, pl.ds(pl.multiple_of(j * 256, 256), 256)] = (
                jnp.dot(gmix[0], half, preferred_element_type=jnp.float32)
                + jnp.dot(gmix[1], half, preferred_element_type=jnp.float32)
            ).astype(jnp.bfloat16)

    for g in range(CHUNKS):
        pltpu.make_async_copy(stage.at[g, others], stage.at[g, others], tok_send.at[g]).wait()
    for slot in range(SLOTS):
        pltpu.make_async_copy(ost.at[slot, others], ost.at[slot, others], ret_send.at[slot]).wait()
    for k in range(3):
        for slot in range(SLOTS):
            to_sibling(k, slot).wait_send()
            if 0 < slot < 7:
                hop(k, slot, slot, up).wait_send()
        last_hop(k).wait_send()

    @pl.when(jnp.logical_not(native))
    def _():
        for k in range(3):
            cross(k).wait_send()


def shards(tokens, chosen, gates, w_gate, w_up, w_down):
    count, width = tokens.shape
    per = chosen.shape[2]
    rows = PEERS * per
    depth, hidden = w_gate.shape[1:]
    vmem = pl.BlockSpec(memory_space=pltpu.VMEM)
    hbm = pl.BlockSpec(memory_space=pl.ANY)
    bf16, f32 = jnp.bfloat16, jnp.float32
    dma = pltpu.SemaphoreType.DMA
    return pl.pallas_call(
        moe_kernel,
        out_shape=jax.ShapeDtypeStruct((count, width), bf16),
        in_specs=[vmem, vmem, vmem, hbm, hbm, hbm],
        out_specs=vmem,
        scratch_shapes=[
            pltpu.VMEM((rows, count), bf16),
            pltpu.VMEM((rows, count), f32),
            pltpu.VMEM((2, count, rows), bf16),
            pltpu.VMEM((CHUNKS, rows, width // CHUNKS), bf16),
            pltpu.VMEM((CHUNKS, rows, width // CHUNKS), bf16),
            pltpu.VMEM((2, SLOTS, 2, depth, hidden), bf16),
            pltpu.VMEM((SLOTS, 2, hidden, depth), bf16),
            pltpu.VMEM((6, rows, hidden // 3), f32),
            pltpu.VMEM((rows, hidden), bf16),
            pltpu.VMEM((SLOTS, rows, width // SLOTS), bf16),
            pltpu.VMEM((SLOTS, rows, width // SLOTS), bf16),
            dma((CHUNKS,)),
            dma((CHUNKS,)),
            dma((SLOTS,)),
            dma((SLOTS,)),
            dma((3, SLOTS)),
            dma((3, SLOTS)),
            dma((3, SLOTS)),
            dma((3, SLOTS)),
            dma((3,)),
        ],
        compiler_params=pltpu.CompilerParams(
            collective_id=0, has_side_effects=True, vmem_limit_bytes=60 * 2**20
        ),
        cost_estimate=pl.CostEstimate(
            flops=11 * 10**9, bytes_accessed=8 * 2**20, transcendentals=rows * hidden
        ),
        name="moe",
    )(tokens, chosen, gates, w_gate, w_up, w_down)


def solution(mesh):
    in_specs = (
        P(("dp", "expert"), None),
        P(("dp", "expert"), None, None),
        P(("dp", "expert"), None, None),
        P("expert", "dp", None),
        P("expert", "dp", None),
        P("expert", None, "dp"),
    )
    out_specs = P(("dp", "expert"), None)
    return jax.shard_map(shards, mesh=mesh, in_specs=in_specs, out_specs=out_specs, check_vma=False)
```

time: 527 us -> 139 us (0.26)
  waiting for transfers between devices: 293 us -> 0 us
  blocking collectives: 163 us -> 0 us
  Pallas kernels: 0 us -> 136 us
  other arithmetic: 26.9 us -> 0 us
  matrix products: 24.9 us -> 0 us
  between operations: 13.1 us -> 0.01 us
    all_gather x3 -> x0, waiting for transfers between devices: 291 us -> none  [the longest x1 117 us: shards(): lax.all_gather(w_up[0], 'dp', axis=0, tiled=True)]
    all_to_all x2 -> x0, blocking collectives: 163 us -> none  [the longest x1 100 us: shards(): lax.all_to_all(expert_out.reshape(experts, per_slab, model_width), 'exper...]
    pallas_call x0 -> x1, Pallas kernels: none -> 136 us  [shards(): pl.pallas_call(moe_kernel, out_shape=jax.ShapeDtypeStruct((count, width),...]
    dot_general x2 -> x0, matrix products: 24.9 us -> none  [the longest x1 17.8 us: shards(): jnp.dot(hidden, lax.all_gather(w_down[0], 'dp', axis=1, tiled=True), pref...]
    scatter-add x1 -> x0, other arithmetic: 16.3 us -> none  [shards(): combined = jnp.zeros((tokens.shape[0], model_width), jnp.float32).at[pick...]
  transfers between devices with their start and end apart: 3 -> 0, of which waited for: 3 -> 0; matrix products, arithmetic and copies ran while one was open for 3% -> 0% of each run, Pallas kernels for 0% -> 0%
where the time goes in v1:
time: 139 us
  Pallas kernels  136 us (98%)
  local copies, waits for them, and re-layouts  3.13 us (2%)
    pallas_call x1, Pallas kernels, shards(): pl.pallas_call(moe_kernel, out_shape=jax.ShapeDtypeStruct((count, width),...  136 us
    unnamed x1, local copies, waits for them, and re-layouts  3.13 us

profile of v1, /device:TPU:1, one launch (start us, length us, event | category | flops | bytes accessed | tf_op | source)
XLA Modules:
  0.0 138.8 jit_solution(8372268634194794077)
XLA Ops:
  0.0 135.6 %moe.1 = bf16[256,4096]{1,0:T(8,128)(2,1)} custom-call(bf16[256,4096]{1,0:T(8,128)(2,1)} %tok.1, s32[1,16,32]{2,1,0:T(8,128)} %cho.1, f32[1,16,32]{2,1,0:T(8,128)} %gat.1, bf16[1,256,768]{2,1,0:T(8,128)(2,1)} %wg.1, bf16[1,256,768]{2,1,0:T(8,128)(2,1)} %wu.1, bf16[1,768,256]{2,1,0:T(8,128)(2,1)} %wd.1), custom_call_target="tpu_custom_call" | custom-call | flops 11000000512 | bytes 8388608 | tf_op jit(solution)/shard_map/moe/pallas_call | solution.py:276
  135.6 3.1 %copy.8 = bf16[256,4096]{1,0:T(8,128)(2,1)} copy(bf16[256,4096]{1,0:T(8,128)(2,1)} %moe.1) | data formatting | bytes 4194304

commit v2 on v1

v2 whole, which is shorter than its diff:
```python
import jax
import jax.numpy as jnp
from jax import lax
from jax.experimental import pallas as pl
from jax.experimental.pallas import tpu as pltpu
from jax.sharding import PartitionSpec as P

MESH = pl.DeviceIdType.MESH
OFFSET = (0, 1, -1, 2, -2, 3, -3, 4)
PEERS = 16
SLOTS = 8
HALVES = 2
GROUPS = ((0,), (1, 2), (3, 4), (5, 6), (7,))


def moe_kernel(
    tok_hbm, cho, gat, wg, wu, wd, o,
    tok, onehot, gcol, gmix, stage, xin, wgu, wdn, acc, hid, ost, ret,
    tok_sem, tok_send, tok_recv, ret_send, ret_recv,
    own_recv, own_send, pair_recv, pair_send, down_recv, down_send, swap_recv, swap_send, first_send, far_send,
):
    dp, ex = lax.axis_index("dp"), lax.axis_index("expert")
    x_hi, z = dp // 8, dp % 8
    y, x_lo, c = ex // 4, (ex // 2) % 2, ex % 2
    x = x_hi * 2 + x_lo
    per = cho.shape[2]
    rows = PEERS * per
    depth, hidden = wg.shape[1:]
    tiles = hidden // 256
    wide = 2 * depth

    def device(xx, yy, zz, cc):
        xx, yy, zz = xx % 4, yy % 4, zz % 8
        return ((xx // 2) * 8 + zz, yy * 4 + (xx % 2) * 2 + cc)

    def shard_columns(slot, q):
        j = q * 8 + (z + OFFSET[slot] + 8) % 8
        return pl.ds(pl.multiple_of(j * depth, depth), depth)

    def remote(src, dst, send, recv, target):
        return pltpu.make_async_remote_copy(
            src_ref=src, dst_ref=dst, send_sem=send, recv_sem=recv, device_id=target,
            device_id_type=MESH,
        )

    up, down = device(x, y, z + 1, c), device(x, y, z + 7, c)
    sibling = device(x, y, z, 1 - c)
    native = c == x_hi

    barrier = pltpu.get_barrier_semaphore()

    def greet(r, carry):
        pl.semaphore_signal(
            barrier, inc=1, device_id=device(x + r % 4, y + r // 4, z, c), device_id_type=MESH
        )
        return carry

    greeted = [(x, y, z + dz, cc) for dz in (1, 7) for cc in range(2)]
    greeted += [(x, y, z, 1 - c), (x + 2, y, z, 1 - c)]
    for other in [device(*there) for there in greeted]:
        pl.semaphore_signal(barrier, inc=1, device_id=other, device_id_type=MESH)
    lax.fori_loop(1, PEERS, greet, 0)

    fetch = pltpu.make_async_copy(tok_hbm, tok, tok_sem.at[0])
    fetch.start()

    near, far = x_hi, 1 - x_hi
    sources = (wg.at[0], wu.at[0])
    half = depth // HALVES

    def rows_of(h):
        return pl.ds(h * half, half)

    for k in range(2):
        for h in range(HALVES):
            start = pltpu.make_async_copy
            part = sources[k].at[rows_of(h)], wgu.at[k, 0, near, rows_of(h)]

            @pl.when(native & (c == k))
            def _():
                start(*part, own_recv.at[near, 0, h]).start()

            @pl.when(native & (c != k))
            def _():
                start(*part, pair_recv.at[near, 0, h]).start()

    @pl.when(native)
    def _():
        pltpu.make_async_copy(wd.at[0], wdn.at[0, c], down_recv.at[0]).start()

    eye = lax.broadcasted_iota(jnp.int32, (per, per), 0) == lax.broadcasted_iota(
        jnp.int32, (per, per), 1
    )
    token_id = lax.broadcasted_iota(jnp.int32, (per, onehot.shape[1]), 1).astype(jnp.float32)
    for r in range(PEERS):
        xx, yy = (x + r % 4) % 4, (y + r // 4) % 4
        e = yy * 4 + (xx % 2) * 2 + xx // 2
        picks = cho[0, pl.ds(e, 1), :].astype(jnp.float32)
        weights = gat[0, pl.ds(e, 1), :]
        pick_col = jnp.sum(jnp.where(eye, picks, 0.0), axis=1, keepdims=True)
        gate_col = jnp.sum(jnp.where(eye, weights, 0.0), axis=1, keepdims=True)
        hit = token_id == pick_col
        onehot[pl.ds(r * per, per), :] = jnp.where(hit, 1.0, 0.0).astype(jnp.bfloat16)
        gcol[pl.ds(r * per, per), :] = jnp.where(hit, gate_col, 0.0)

    pl.semaphore_wait(barrier, PEERS - 1 + len(greeted))

    def near_first(k, h, there):
        slot, index = (2, 0) if there == 1 else (1, 1)
        return remote(
            sources[k].at[rows_of(h)], wgu.at[k, slot, near, rows_of(h)],
            first_send.at[index, k, h], own_recv.at[near, slot, h], device(x, y, z + there, k),
        )

    def near_sibling(k, h, semaphores):
        return remote(
            sources[k].at[rows_of(h)], wgu.at[k, 0, near, rows_of(h)],
            first_send.at[2, k, h], semaphores.at[near, 0, h], sibling,
        )

    def far_first(k, h):
        return remote(
            sources[k].at[rows_of(h)], wgu.at[k, 0, x_hi, rows_of(h)],
            first_send.at[0, k, h], own_recv.at[x_hi, 0, h], device(x + 2, y, z, k),
        )

    def near_firsts(act):
        for h in range(HALVES):
            for k in range(2):
                act(near_first(k, h, 1))
                act(near_first(k, h, 7))
        for h in range(HALVES):
            for k in range(2):

                @pl.when(c == k)
                def _():
                    act(near_sibling(k, h, pair_recv))

                @pl.when(c != k)
                def _():
                    act(near_sibling(k, h, own_recv))

    def far_firsts(act):
        for h in range(HALVES):
            for k in range(2):
                act(far_first(k, h))

    def far_down():
        return remote(
            wd.at[0], wdn.at[0, 1 - c], far_send.at[0], down_recv.at[0],
            device(x + 2, y, z, 1 - c),
        )

    @pl.when(native)
    def _():
        near_firsts(lambda copy: copy.start())

    @pl.when(jnp.logical_not(native))
    def _():
        far_firsts(lambda copy: copy.start())

    def arrived(slot, q, h):
        part = wgu.at[c, slot, q, rows_of(h)]
        pltpu.make_async_copy(part, part, own_recv.at[q, slot, h]).wait()

    def pair(slot, q, h):
        part = wgu.at[c, slot, q, rows_of(h)]
        return remote(part, part, pair_send.at[q, slot, h], pair_recv.at[q, slot, h], sibling)

    def from_pair(slot, q, h):
        part = wgu.at[1 - c, slot, q, rows_of(h)]
        pltpu.make_async_copy(part, part, pair_recv.at[q, slot, h]).wait()

    def hop(src, dst, q, h, target):
        return remote(
            wgu.at[c, src, q, rows_of(h)], wgu.at[c, dst, q, rows_of(h)], own_send.at[q, dst, h],
            own_recv.at[q, dst, h], target,
        )

    def down_arrived(slot):
        part = wdn.at[slot, c]
        pltpu.make_async_copy(part, part, down_recv.at[slot]).wait()

    def swap(slot):
        part = wdn.at[slot, c]
        return remote(part, part, swap_send.at[slot], swap_recv.at[slot], sibling)

    def from_swap(slot):
        part = wdn.at[slot, 1 - c]
        pltpu.make_async_copy(part, part, swap_recv.at[slot]).wait()

    def down_hop(src, dst, target):
        return remote(
            wdn.at[src, c], wdn.at[dst, c], down_send.at[dst], down_recv.at[dst], target
        )

    last_src, last_target = 6 - c, device(x, y, z + 1 + 6 * c, c)

    def onward(slot, send):
        if slot == 0:
            send(0, 2, up)
            send(0, 1, down)
        elif slot in (1, 3):
            send(slot, slot + 2, down)
        elif slot in (2, 4):
            send(slot, slot + 2, up)
        elif slot in (5, 6):

            @pl.when(last_src == slot)
            def _():
                send(slot, 7, last_target)

    def spread(slot, q, h):
        arrived(slot, q, h)
        onward(slot, lambda src, dst, target: hop(src, dst, q, h, target).start())
        pair(slot, q, h).start()

    def columns(group):
        return pl.ds(group[0] * wide, len(group) * wide)

    def token_block(ref, group, r):
        return ref.at[pl.ds(pl.multiple_of(r * per, per), per), columns(group)]

    def send_tokens(g):
        group = GROUPS[g]
        for slot in group:
            for q in range(2):
                stage[:, pl.ds(slot * wide + q * depth, depth)] = jnp.dot(
                    onehot[...], tok[:, shard_columns(slot, q)], preferred_element_type=jnp.float32
                ).astype(jnp.bfloat16)

        def send(r, carry):
            remote(
                token_block(stage, group, r), token_block(xin, group, r), tok_send.at[g],
                tok_recv.at[g], device(x + r % 4, y + r // 4, z, c),
            ).start()
            return carry

        lax.fori_loop(1, PEERS, send, 0)
        xin[pl.ds(0, per), columns(group)] = stage[pl.ds(0, per), columns(group)]

    def spread_group(g, q, h):
        for slot in GROUPS[g]:
            spread(slot, q, h)

    fetch.wait()
    send_tokens(0)
    spread_group(0, far, 0)
    spread_group(1, near, 0)
    send_tokens(1)
    spread_group(0, far, 1)
    spread_group(1, near, 1)
    for g in range(2, len(GROUPS)):
        send_tokens(g)

    @pl.when(jnp.logical_not(native))
    def _():
        far_down().start()

    mixed = gcol[...].T
    high = mixed.astype(jnp.bfloat16)
    gmix[0] = high
    gmix[1] = (mixed - high.astype(jnp.float32)).astype(jnp.bfloat16)

    others = pl.ds(per, rows - per)

    def add_products(g):
        group = GROUPS[g]
        for q in (near, far):
            for slot in group:
                for h in range(HALVES):
                    from_pair(slot, q, h)
        if g == 0:
            for h in range(HALVES):
                arrived(0, near, h)
        block = xin.at[others, columns(group)]
        pltpu.make_async_copy(block, block, tok_recv.at[g]).wait()

        def multiply(n, carry):
            k, tile = n // tiles, n % tiles
            part = wgu[
                k, pl.ds(group[0], len(group)), :, :, pl.ds(pl.multiple_of(tile * 256, 256), 256)
            ]
            product = jnp.dot(
                xin[:, columns(group)], part.reshape(len(group) * wide, 256),
                preferred_element_type=jnp.float32,
            )
            if g == 0:
                acc[n] = product
            else:
                acc[n] += product
            return carry

        lax.fori_loop(0, 2 * tiles, multiply, 0)

    for g in range(2, len(GROUPS)):
        for h in range(HALVES):
            spread_group(g - 1, far, h)
            spread_group(g, near, h)
        add_products(g - 2)
        if g == 3:
            down_arrived(0)
            swap(0).start()
    add_products(3)
    for h in range(HALVES):
        spread_group(4, far, h)
    onward(0, lambda src, dst, target: down_hop(src, dst, target).start())
    add_products(4)

    for tile in range(tiles):
        gate_part = acc[tile]
        hid[:, pl.ds(tile * 256, 256)] = (
            gate_part / (1.0 + jnp.exp(-gate_part)) * acc[tiles + tile]
        ).astype(jnp.bfloat16)

    for slot in range(SLOTS):
        if slot > 0:
            down_arrived(slot)
            onward(slot, lambda src, dst, target: down_hop(src, dst, target).start())
            swap(slot).start()
        from_swap(slot)
        for q in range(2):
            ost[slot, :, pl.ds(q * depth, depth)] = jnp.dot(
                hid[...], wdn[slot, q], preferred_element_type=jnp.float32
            ).astype(jnp.bfloat16)

        def give_back(r, carry):
            block = pl.ds(pl.multiple_of(r * per, per), per)
            remote(
                ost.at[slot, block], ret.at[slot, block], ret_send.at[slot], ret_recv.at[slot],
                device(x + 4 - r % 4, y + 4 - r // 4, z, c),
            ).start()
            return carry

        lax.fori_loop(1, PEERS, give_back, 0)
        ret[slot, pl.ds(0, per), :] = ost[slot, pl.ds(0, per), :]

    for slot in range(SLOTS):
        block = ret.at[slot, others]
        pltpu.make_async_copy(block, block, ret_recv.at[slot]).wait()
        for q in range(2):
            part = ret[slot, :, pl.ds(q * depth, depth)]
            o[:, shard_columns(slot, q)] = (
                jnp.dot(gmix[0], part, preferred_element_type=jnp.float32)
                + jnp.dot(gmix[1], part, preferred_element_type=jnp.float32)
            ).astype(jnp.bfloat16)

    for g, group in enumerate(GROUPS):
        block = stage.at[others, columns(group)]
        pltpu.make_async_copy(block, block, tok_send.at[g]).wait()
    for slot in range(SLOTS):
        block = ost.at[slot, others]
        pltpu.make_async_copy(block, block, ret_send.at[slot]).wait()
        swap(slot).wait_send()
        for h in range(HALVES):
            for q in (near, far):
                if slot > 0 or q is far:
                    pair(slot, q, h).wait_send()
                if slot > 2 or (slot > 0 and q is far):
                    hop(0, slot, q, h, up).wait_send()
        if slot > 0:
            down_hop(0, slot, up).wait_send()
    @pl.when(native)
    def _():
        near_firsts(lambda copy: copy.wait_send())

    @pl.when(jnp.logical_not(native))
    def _():
        far_firsts(lambda copy: copy.wait_send())
        far_down().wait_send()


def shards(tokens, chosen, gates, w_gate, w_up, w_down):
    count, width = tokens.shape
    per = chosen.shape[2]
    rows = PEERS * per
    depth, hidden = w_gate.shape[1:]
    vmem = pl.BlockSpec(memory_space=pltpu.VMEM)
    hbm = pl.BlockSpec(memory_space=pl.ANY)
    bf16, f32 = jnp.bfloat16, jnp.float32
    dma = pltpu.SemaphoreType.DMA
    return pl.pallas_call(
        moe_kernel,
        out_shape=pltpu.VMEM((count, width), bf16),
        in_specs=[hbm, vmem, vmem, hbm, hbm, hbm],
        out_specs=vmem,
        scratch_shapes=[
            pltpu.VMEM((count, width), bf16),
            pltpu.VMEM((rows, count), bf16),
            pltpu.VMEM((rows, count), f32),
            pltpu.VMEM((2, count, rows), bf16),
            pltpu.VMEM((rows, width), bf16),
            pltpu.VMEM((rows, width), bf16),
            pltpu.VMEM((2, SLOTS, 2, depth, hidden), bf16),
            pltpu.VMEM((SLOTS, 2, hidden, depth), bf16),
            pltpu.VMEM((2 * hidden // 256, rows, 256), f32),
            pltpu.VMEM((rows, hidden), bf16),
            pltpu.VMEM((SLOTS, rows, width // SLOTS), bf16),
            pltpu.VMEM((SLOTS, rows, width // SLOTS), bf16),
            dma((1,)),
            dma((len(GROUPS),)),
            dma((len(GROUPS),)),
            dma((SLOTS,)),
            dma((SLOTS,)),
            dma((2, SLOTS, HALVES)),
            dma((2, SLOTS, HALVES)),
            dma((2, SLOTS, HALVES)),
            dma((2, SLOTS, HALVES)),
            dma((SLOTS,)),
            dma((SLOTS,)),
            dma((SLOTS,)),
            dma((SLOTS,)),
            dma((3, 2, HALVES)),
            dma((1,)),
        ],
        compiler_params=pltpu.CompilerParams(
            collective_id=0, has_side_effects=True, vmem_limit_bytes=61 * 2**20
        ),
        cost_estimate=pl.CostEstimate(
            flops=11 * 10**9, bytes_accessed=8 * 2**20, transcendentals=rows * hidden
        ),
        name="moe",
    )(tokens, chosen, gates, w_gate, w_up, w_down)


def solution(mesh):
    in_specs = (
        P(("dp", "expert"), None),
        P(("dp", "expert"), None, None),
        P(("dp", "expert"), None, None),
        P("expert", "dp", None),
        P("expert", "dp", None),
        P("expert", None, "dp"),
    )
    out_specs = P(("dp", "expert"), None)
    return jax.shard_map(shards, mesh=mesh, in_specs=in_specs, out_specs=out_specs, check_vma=False)
```

time: 139 us -> 135 us (0.971)
  Pallas kernels: 136 us -> 133 us
  local copies, waits for them, and re-layouts: 3.13 us -> 1.32 us
    pallas_call x1, Pallas kernels: 136 us -> 133 us  [shards(): pl.pallas_call(moe_kernel, out_shape=pltpu.VMEM((count, width), bf16), in...]
    unnamed x1, local copies, waits for them, and re-layouts: 3.13 us -> 1.32 us
where the time goes in v2:
time: 135 us
  Pallas kernels  133 us (99%)
    pallas_call x1, Pallas kernels, shards(): pl.pallas_call(moe_kernel, out_shape=pltpu.VMEM((count, width), bf16), in...  133 us

profile of v2, /device:TPU:1, one launch (start us, length us, event | category | flops | bytes accessed | tf_op | source)
XLA Modules:
  0.0 134.8 jit_solution(17648013240386218128)
XLA Ops:
  0.0 133.4 %moe.1 = bf16[256,4096]{1,0:T(8,128)(2,1)S(1)} custom-call(bf16[256,4096]{1,0:T(8,128)(2,1)} %tok_hbm.1, s32[1,16,32]{2,1,0:T(8,128)} %cho.1, f32[1,16,32]{2,1,0:T(8,128)} %gat.1, bf16[1,256,768]{2,1,0:T(8,128)(2,1)} %wg.1, bf16[1,256,768]{2,1,0:T(8,128)(2,1)} %wu.1, bf16[1,768,256]{2,1,0:T(8,128)(2,1)} %wd.1), custom_call_target="tpu_custom_call" | custom-call | flops 11000000512 | bytes 8388608 | tf_op jit(solution)/shard_map/moe/pallas_call | solution.py:382
  133.4 1.3 copy.8

commit v3 on v2

--- a/solution.py
+++ b/solution.py
@@ -264,7 +264,7 @@
 
     others = pl.ds(per, rows - per)
 
-    def add_products(g):
+    def products_ready(g):
         group = GROUPS[g]
         for q in (near, far):
             for slot in group:
@@ -276,48 +276,54 @@
         block = xin.at[others, columns(group)]
         pltpu.make_async_copy(block, block, tok_recv.at[g]).wait()
 
+    def product(g, k, lanes):
+        group = GROUPS[g]
+        part = wgu[k, pl.ds(group[0], len(group)), :, :, lanes]
+        return jnp.dot(
+            xin[:, columns(group)], part.reshape(len(group) * wide, 256),
+            preferred_element_type=jnp.float32,
+        )
+
+    def add_products(g):
+        products_ready(g)
+
         def multiply(n, carry):
             k, tile = n // tiles, n % tiles
-            part = wgu[
-                k, pl.ds(group[0], len(group)), :, :, pl.ds(pl.multiple_of(tile * 256, 256), 256)
-            ]
-            product = jnp.dot(
-                xin[:, columns(group)], part.reshape(len(group) * wide, 256),
-                preferred_element_type=jnp.float32,
-            )
+            more = product(g, k, pl.ds(pl.multiple_of(tile * 256, 256), 256))
             if g == 0:
-                acc[n] = product
+                acc[n] = more
             else:
-                acc[n] += product
+                acc[n] += more
             return carry
 
         lax.fori_loop(0, 2 * tiles, multiply, 0)
+
+    def make_hidden(g):
+        products_ready(g)
+        for tile in range(tiles):
+            lanes = pl.ds(tile * 256, 256)
+            gate_part = acc[tile] + product(g, 0, lanes)
+            up_part = acc[tiles + tile] + product(g, 1, lanes)
+            hid[:, lanes] = (gate_part / (1.0 + jnp.exp(-gate_part)) * up_part).astype(jnp.bfloat16)
 
     for g in range(2, len(GROUPS)):
         for h in range(HALVES):
             spread_group(g - 1, far, h)
             spread_group(g, near, h)
         add_products(g - 2)
-        if g == 3:
-            down_arrived(0)
-            swap(0).start()
     add_products(3)
     for h in range(HALVES):
         spread_group(4, far, h)
+    down_arrived(0)
     onward(0, lambda src, dst, target: down_hop(src, dst, target).start())
-    add_products(4)
-
-    for tile in range(tiles):
-        gate_part = acc[tile]
-        hid[:, pl.ds(tile * 256, 256)] = (
-            gate_part / (1.0 + jnp.exp(-gate_part)) * acc[tiles + tile]
-        ).astype(jnp.bfloat16)
+    swap(0).start()
+    make_hidden(4)
 
     for slot in range(SLOTS):
-        if slot > 0:
-            down_arrived(slot)
-            onward(slot, lambda src, dst, target: down_hop(src, dst, target).start())
-            swap(slot).start()
+        for fresh in next((g for g in GROUPS[1:] if g[0] == slot), ()):
+            down_arrived(fresh)
+            onward(fresh, lambda src, dst, target: down_hop(src, dst, target).start())
+            swap(fresh).start()
         from_swap(slot)
         for q in range(2):
             ost[slot, :, pl.ds(q * depth, depth)] = jnp.dot(

time: 135 us -> 132 us (0.978)
  Pallas kernels: 133 us -> 130 us
    pallas_call x1, Pallas kernels: 133 us -> 130 us  [shards(): pl.pallas_call(moe_kernel, out_shape=pltpu.VMEM((count, width), bf16), in...]
where the time goes in v3:
time: 132 us
  Pallas kernels  130 us (98%)
  local copies, waits for them, and re-layouts  1.32 us (1%)
    pallas_call x1, Pallas kernels, shards(): pl.pallas_call(moe_kernel, out_shape=pltpu.VMEM((count, width), bf16), in...  130 us

profile of v3, /device:TPU:1, one launch (start us, length us, event | category | flops | bytes accessed | tf_op | source)
XLA Modules:
  0.0 131.6 jit_solution(9606798982256100642)
XLA Ops:
  0.0 130.3 %moe.1 = bf16[256,4096]{1,0:T(8,128)(2,1)S(1)} custom-call(bf16[256,4096]{1,0:T(8,128)(2,1)} %tok_hbm.1, s32[1,16,32]{2,1,0:T(8,128)} %cho.1, f32[1,16,32]{2,1,0:T(8,128)} %gat.1, bf16[1,256,768]{2,1,0:T(8,128)(2,1)} %wg.1, bf16[1,256,768]{2,1,0:T(8,128)(2,1)} %wu.1, bf16[1,768,256]{2,1,0:T(8,128)(2,1)} %wd.1), custom_call_target="tpu_custom_call" | custom-call | flops 11000000512 | bytes 8388608 | tf_op jit(solution)/shard_map/moe/pallas_call | solution.py:388
  130.3 1.3 %copy.8 = bf16[256,4096]{1,0:T(8,128)(2,1)} copy(bf16[256,4096]{1,0:T(8,128)(2,1)S(1)} %moe.1) | data formatting | bytes 4194304

commit v4 on v3

--- a/solution.py
+++ b/solution.py
@@ -306,17 +306,20 @@
             up_part = acc[tiles + tile] + product(g, 1, lanes)
             hid[:, lanes] = (gate_part / (1.0 + jnp.exp(-gate_part)) * up_part).astype(jnp.bfloat16)
 
+    ready = {(2, 1): 0, (3, 0): 1, (3, 1): 2}
     for g in range(2, len(GROUPS)):
         for h in range(HALVES):
             spread_group(g - 1, far, h)
             spread_group(g, near, h)
-        add_products(g - 2)
+            if (g, h) in ready:
+                add_products(ready[g, h])
     add_products(3)
     for h in range(HALVES):
         spread_group(4, far, h)
-    down_arrived(0)
-    onward(0, lambda src, dst, target: down_hop(src, dst, target).start())
-    swap(0).start()
+        if h == 0:
+            down_arrived(0)
+            onward(0, lambda src, dst, target: down_hop(src, dst, target).start())
+            swap(0).start()
     make_hidden(4)
 
     for slot in range(SLOTS):

time: 132 us -> 129 us (0.977)
  Pallas kernels: 130 us -> 128 us
    pallas_call x1, Pallas kernels: 130 us -> 128 us  [shards(): pl.pallas_call(moe_kernel, out_shape=pltpu.VMEM((count, width), bf16), in...]
where the time goes in v4:
time: 129 us
  Pallas kernels  128 us (99%)
  local copies, waits for them, and re-layouts  1.32 us (1%)
    pallas_call x1, Pallas kernels, shards(): pl.pallas_call(moe_kernel, out_shape=pltpu.VMEM((count, width), bf16), in...  128 us

profile of v4, /device:TPU:1, one launch (start us, length us, event | category | flops | bytes accessed | tf_op | source)
XLA Modules:
  0.0 128.9 jit_solution(13185064001843383398)
XLA Ops:
  0.0 127.5 %moe.1 = bf16[256,4096]{1,0:T(8,128)(2,1)S(1)} custom-call(bf16[256,4096]{1,0:T(8,128)(2,1)} %tok_hbm.1, s32[1,16,32]{2,1,0:T(8,128)} %cho.1, f32[1,16,32]{2,1,0:T(8,128)} %gat.1, bf16[1,256,768]{2,1,0:T(8,128)(2,1)} %wg.1, bf16[1,256,768]{2,1,0:T(8,128)(2,1)} %wu.1, bf16[1,768,256]{2,1,0:T(8,128)(2,1)} %wd.1), custom_call_target="tpu_custom_call" | custom-call | flops 11000000512 | bytes 8388608 | tf_op jit(solution)/shard_map/moe/pallas_call | solution.py:391
  127.5 1.3 %copy.8 = bf16[256,4096]{1,0:T(8,128)(2,1)} copy(bf16[256,4096]{1,0:T(8,128)(2,1)S(1)} %moe.1) | data formatting | bytes 4194304

commit v5 on v4

--- a/solution.py
+++ b/solution.py
@@ -257,11 +257,6 @@
     def _():
         far_down().start()
 
-    mixed = gcol[...].T
-    high = mixed.astype(jnp.bfloat16)
-    gmix[0] = high
-    gmix[1] = (mixed - high.astype(jnp.float32)).astype(jnp.bfloat16)
-
     others = pl.ds(per, rows - per)
 
     def products_ready(g):
@@ -343,6 +338,11 @@
 
         lax.fori_loop(1, PEERS, give_back, 0)
         ret[slot, pl.ds(0, per), :] = ost[slot, pl.ds(0, per), :]
+
+    mixed = gcol[...].T
+    high = mixed.astype(jnp.bfloat16)
+    gmix[0] = high
+    gmix[1] = (mixed - high.astype(jnp.float32)).astype(jnp.bfloat16)
 
     for slot in range(SLOTS):
         block = ret.at[slot, others]

time: 129 us -> 129 us (level)
  no operation moved by 1% of the time
where the time goes in v5:
time: 129 us
  Pallas kernels  128 us (99%)
  local copies, waits for them, and re-layouts  1.32 us (1%)
    pallas_call x1, Pallas kernels, shards(): pl.pallas_call(moe_kernel, out_shape=pltpu.VMEM((count, width), bf16), in...  128 us

profile of v5, /device:TPU:1, one launch (start us, length us, event | category | flops | bytes accessed | tf_op | source)
XLA Modules:
  0.0 128.9 jit_solution(14340659620036769477)
XLA Ops:
  0.0 127.5 %moe.1 = bf16[256,4096]{1,0:T(8,128)(2,1)S(1)} custom-call(bf16[256,4096]{1,0:T(8,128)(2,1)} %tok_hbm.1, s32[1,16,32]{2,1,0:T(8,128)} %cho.1, f32[1,16,32]{2,1,0:T(8,128)} %gat.1, bf16[1,256,768]{2,1,0:T(8,128)(2,1)} %wg.1, bf16[1,256,768]{2,1,0:T(8,128)(2,1)} %wu.1, bf16[1,768,256]{2,1,0:T(8,128)(2,1)} %wd.1), custom_call_target="tpu_custom_call" | custom-call | flops 11000000512 | bytes 8388608 | tf_op jit(solution)/shard_map/moe/pallas_call | solution.py:391
  127.5 1.3 %copy.8 = bf16[256,4096]{1,0:T(8,128)(2,1)} copy(bf16[256,4096]{1,0:T(8,128)(2,1)S(1)} %moe.1) | data formatting | bytes 4194304
